TPU v7x, 128 devices: a whole 4x4x4 slice. The times are simulated.
128 devices in a mesh: tensor: 4 (over y), ctx: 16 (over x_hi, z, core), section: 2 (over x_lo).
Axes of the slice: x: 4 (x_hi: 2, x_lo: 2; x = x_hi * 2 + x_lo), y: 4, z: 4, core: 2. Of those that a mesh axis runs over, the one named last changes fastest.
Arguments:
- segment_query: bfloat16 [4096, 8192], P('ctx', ('tensor', 'section')), may hold values from -64 to 64
- segment_key_value: bfloat16 [4096, 2048], P('ctx', ('tensor', 'section')), may hold values from -64 to 64
- earlier_key_value: bfloat16 [4096, 2048], P('ctx', ('tensor', 'section')), may hold values from -6 to 6
- fill_start: int32 [1], replicated, may hold values from 2048 to 4096
- block_page: int32 [64], replicated, may hold values from 0 to 63, each once
- decode_query: bfloat16 [256, 4, 8192], P('ctx', None, ('tensor', 'section')), may hold values from -64 to 64
- decode_key_value: bfloat16 [256, 4, 2048], P('ctx', None, ('tensor', 'section')), may hold values from -64 to 64
- cached_key_value: bfloat16 [256, 1024, 2048], P(('ctx', 'section'), None, 'tensor'), may hold values from -6 to 6
- cache_length: int32 [256], P(('ctx', 'section')), may hold values from 1 to 1024, 131072 in all
Outputs:
- fill_output: bfloat16 [4096, 8192], P('ctx', ('tensor', 'section'))
- shipped_pages: bfloat16 [64, 64, 2048], P(('ctx', 'section'), None, 'tensor')
- step_output: bfloat16 [256, 4, 8192], P(('ctx', 'section'), None, 'tensor')
Inputs may be any that keep to these rules, and one draw needn't show every extreme that they name: `block_page`: each page is named by exactly one block. `cache_length`: some row has exactly 1024.
All inputs are finite; a program needn't handle non-finite values. No bound on the sum of `cache_length` on one device may be relied on, other than what follows from the above.
Results may differ from a plain program's by a relative error of at most 0.01.
Values may be sent and summed in bfloat16 or wider, within the bound.
A program may use at most 128 MiB of HBM per device.

v0:
```python
import math

import jax
import jax.numpy as jnp
from jax import lax
from jax.sharding import PartitionSpec as P

QUERY_HEADS = 64
KEYVALUE_HEADS = 8
HEAD_SIZE = 128
PAGE_TOKENS = 64


theta_base = 500000.0
neg_big = -1e30


def apply_rotary(vectors, position):
    half_width = vectors.shape[-1] // 2
    frequency = theta_base ** (
        -(jnp.arange(half_width).astype(jnp.float32) * 2.0 / vectors.shape[-1])
    )
    angles = position[..., None] * frequency
    cosine = jnp.cos(angles)
    sine_part = jnp.sin(angles)
    first_half = vectors[..., :half_width]
    second_half = vectors[..., half_width:]
    return jnp.concatenate(
        [
            first_half * cosine - second_half * sine_part,
            second_half * cosine + first_half * sine_part,
        ],
        -1,
    )


def pick_rows(held_rows, shard_rows, global_rows):
    row_count = shard_rows.shape[0]
    inside = (global_rows >= 0) & (global_rows < row_count)
    taken = shard_rows[jnp.clip(global_rows, 0, row_count - 1)]
    return jnp.where(inside[..., None], taken, held_rows)


def on_device(
    segment_query,
    segment_key_value,
    earlier_key_value,
    fill_start,
    block_page,
    decode_query,
    decode_key_value,
    cached_key_value,
    cache_length,
):
    query_group_count = QUERY_HEADS // KEYVALUE_HEADS
    score_scale = 1.0 / math.sqrt(HEAD_SIZE)
    token_count = segment_query.shape[0]
    prior_count = earlier_key_value.shape[0]
    span_rows = token_count + prior_count
    row_width = segment_key_value.shape[1]
    local_heads = row_width // (2 * HEAD_SIZE)
    ctx_index = lax.axis_index("ctx")
    section_index = lax.axis_index("section")
    section_count = lax.axis_size("section")
    ctx_count = lax.axis_size("ctx")
    block_total = block_page.shape[0]
    pages_local = block_total // (ctx_count * section_count)
    start_pos = fill_start[0]
    token_positions = start_pos + ctx_index * token_count + jnp.arange(token_count, dtype=jnp.int32)
    rotated_queries = apply_rotary(
        segment_query.astype(jnp.float32).reshape(
            token_count, local_heads, query_group_count, HEAD_SIZE
        ),
        token_positions[:, None, None].astype(jnp.float32),
    ).astype(jnp.bfloat16)
    fresh_entries = segment_key_value.reshape(token_count, local_heads, 2, HEAD_SIZE)
    rotated_keys = apply_rotary(
        fresh_entries[:, :, 0].astype(jnp.float32), token_positions[:, None].astype(jnp.float32)
    ).astype(jnp.bfloat16)
    finished_rows = jnp.stack([rotated_keys, fresh_entries[:, :, 1]], 2).reshape(
        token_count, row_width
    )
    context = jnp.concatenate([earlier_key_value, finished_rows], 0)

    def attend_block(running, block_keys, block_values, key_pos, key_usable):
        running_max, weight_sum, weighted = running
        scores = (
            jnp.einsum(
                "thgd,shd->thgs", rotated_queries, block_keys, preferred_element_type=jnp.float32
            )
            * score_scale
        )
        allowed = ((key_pos[None, :] <= token_positions[:, None]) & key_usable[None, :])[
            :, None, None, :
        ]
        scores = jnp.where(allowed, scores, neg_big)
        new_max = jnp.maximum(running_max, jnp.max(scores, -1))
        weights = jnp.where(allowed, jnp.exp(scores - new_max[..., None]), 0.0)
        factor = jnp.exp(running_max - new_max)
        weight_sum = weight_sum * factor + jnp.sum(weights, -1)
        weighted = weighted * factor[..., None] + jnp.einsum(
            "thgs,shd->thgd",
            weights.astype(jnp.bfloat16),
            block_values,
            preferred_element_type=jnp.float32,
        )
        return (new_max, weight_sum, weighted)

    start_state = (
        jnp.full((token_count, local_heads, query_group_count), neg_big, jnp.float32),
        jnp.zeros((token_count, local_heads, query_group_count), jnp.float32),
        jnp.zeros((token_count, local_heads, query_group_count, HEAD_SIZE), jnp.float32),
    )
    fold_init = (start_state, jnp.zeros((1,), jnp.bfloat16))
    running = fold_init[0]
    shard_rows = lax.all_gather(context, "ctx", axis=0, tiled=True)
    row_count = shard_rows.shape[0]
    block_rows = math.gcd(row_count, 512)
    block_count = row_count // block_rows
    page_listing = shard_rows.reshape(block_count, block_rows, local_heads, 2, HEAD_SIZE)
    firsts = jnp.arange(block_count, dtype=jnp.int32) * block_rows

    def block_step(inner_state, packed):
        block_data, block_first = packed
        global_rows = block_first + jnp.arange(block_rows, dtype=jnp.int32)
        owner = global_rows // span_rows
        local_row = global_rows % span_rows
        is_prior = local_row < prior_count
        key_pos = jnp.where(
            is_prior,
            owner * prior_count + local_row,
            start_pos + owner * token_count + local_row - prior_count,
        )
        key_usable = jnp.logical_or(jnp.logical_not(is_prior), key_pos < start_pos)
        return (
            attend_block(
                inner_state, block_data[:, :, 0], block_data[:, :, 1], key_pos, key_usable
            ),
            None,
        )

    running, unused = lax.scan(block_step, running, (page_listing, firsts))
    running_max, weight_sum, weighted = running
    fill_output = (
        (weighted / weight_sum[..., None])
        .reshape(token_count, local_heads * query_group_count * HEAD_SIZE)
        .astype(jnp.bfloat16)
    )
    both_heads = lax.all_gather(finished_rows, "section", axis=1, tiled=True)
    page_ids = (
        jnp.reshape(ctx_index * section_count + section_index, (1,))[:, None] * pages_local
        + jnp.arange(pages_local, dtype=jnp.int32)[None, :]
    )
    matches = (block_page[None, None, :] == page_ids[:, :, None]).astype(jnp.int32)
    own_rows = (
        jnp.sum(matches * jnp.arange(block_total, dtype=jnp.int32)[None, None, :], -1) * PAGE_TOKENS
    )[0][:, None] + jnp.arange(PAGE_TOKENS, dtype=jnp.int32)[None, :]
    empty_pages = jnp.zeros((pages_local, PAGE_TOKENS, section_count * row_width), jnp.bfloat16)
    shipped_pages = pick_rows(
        empty_pages, lax.all_gather(both_heads, "ctx", axis=0, tiled=True), own_rows
    )
    fresh_query, fresh_keyval = (
        lax.all_to_all(decode_query, "section", split_axis=0, concat_axis=2, tiled=True),
        lax.all_to_all(decode_key_value, "section", split_axis=0, concat_axis=2, tiled=True),
    )
    row_count = fresh_query.shape[0]
    step_count = fresh_query.shape[1]
    decode_heads = fresh_keyval.shape[2] // (2 * HEAD_SIZE)
    slot_count = cached_key_value.shape[1]
    decode_positions = cache_length[:, None] + jnp.arange(step_count, dtype=jnp.int32)[None, :]
    decode_rotated = apply_rotary(
        fresh_query.astype(jnp.float32).reshape(
            row_count, step_count, decode_heads, query_group_count, HEAD_SIZE
        ),
        decode_positions[:, :, None, None].astype(jnp.float32),
    ).astype(jnp.bfloat16)
    decode_fresh_entries = fresh_keyval.reshape(row_count, step_count, decode_heads, 2, HEAD_SIZE)
    step_key = apply_rotary(
        decode_fresh_entries[:, :, :, 0].astype(jnp.float32),
        decode_positions[:, :, None].astype(jnp.float32),
    ).astype(jnp.bfloat16)
    step_values = decode_fresh_entries[:, :, :, 1]
    cache_entries = cached_key_value.reshape(row_count, slot_count, decode_heads, 2, HEAD_SIZE)
    old_ok = jnp.arange(slot_count, dtype=jnp.int32)[None, :] < cache_length[:, None]
    old_ok = old_ok[:, None, None, None, :]
    step_index = jnp.arange(step_count, dtype=jnp.int32)
    new_ok = (step_index[None, :] <= step_index[:, None])[None, :, None, None, :]
    old_scores = (
        jnp.einsum(
            "rjhgd,rchd->rjhgc",
            decode_rotated,
            cache_entries[:, :, :, 0],
            preferred_element_type=jnp.float32,
        )
        * score_scale
    )
    new_scores = (
        jnp.einsum(
            "rjhgd,rkhd->rjhgk", decode_rotated, step_key, preferred_element_type=jnp.float32
        )
        * score_scale
    )
    old_scores = jnp.where(old_ok, old_scores, neg_big)
    new_scores = jnp.where(new_ok, new_scores, neg_big)
    row_max = jnp.maximum(
        jnp.max(old_scores, -1, keepdims=True), jnp.max(new_scores, -1, keepdims=True)
    )
    old_weights = jnp.where(old_ok, jnp.exp(old_scores - row_max), 0.0)
    new_weights = jnp.where(new_ok, jnp.exp(new_scores - row_max), 0.0)
    step_total = jnp.sum(old_weights, -1) + jnp.sum(new_weights, -1)
    mixed = jnp.einsum(
        "rjhgc,rchd->rjhgd",
        old_weights.astype(jnp.bfloat16),
        cache_entries[:, :, :, 1],
        preferred_element_type=jnp.float32,
    )
    mixed = mixed + jnp.einsum(
        "rjhgk,rkhd->rjhgd",
        new_weights.astype(jnp.bfloat16),
        step_values,
        preferred_element_type=jnp.float32,
    )
    step_output = (
        (mixed / step_total[..., None])
        .reshape(row_count, step_count, decode_heads * query_group_count * HEAD_SIZE)
        .astype(jnp.bfloat16)
    )
    return (fill_output, shipped_pages, step_output)


def solution(mesh):
    in_specs = (
        P("ctx", ("tensor", "section")),
        P("ctx", ("tensor", "section")),
        P("ctx", ("tensor", "section")),
        P(),
        P(),
        P("ctx", None, ("tensor", "section")),
        P("ctx", None, ("tensor", "section")),
        P(("ctx", "section"), None, "tensor"),
        P(("ctx", "section")),
    )
    out_specs = (
        P("ctx", ("tensor", "section")),
        P(("ctx", "section"), None, "tensor"),
        P(("ctx", "section"), None, "tensor"),
    )
    return jax.shard_map(
        on_device, mesh=mesh, in_specs=in_specs, out_specs=out_specs, check_vma=False
    )
```

profile of v0, /device:TPU:1, one launch (start us, length us, event | category | flops | bytes accessed | tf_op | source)
XLA Modules:
  0.0 287.0 jit_solution(11971435453934119884)
XLA Ops:
  15.2 5.8 %all_gather.10 = bf16[256,512]{1,0:T(8,128)(2,1)} all-gather(bf16[256,256]{1,0:T(8,128)(2,1)S(1)} %bitcast.189), channel_id=1, replica_groups=mesh['tensor'=4,'ctx'=16,'section'=2] {'section'}, dimensions={1}, use_global_device_ids=true | all-gather | bytes 393216 | tf_op jit(solution)/shard_map/all_gather | solution.py:149
  24.9 11.6 %copy.42 = bf16[8,1024,512]{1,2,0:T(8,128)(2,1)} copy(bf16[8,1024,512]{2,1,0:T(8,128)(2,1)} %param.18) | data formatting | bytes 16777216 | tf_op args[7]
  36.5 3.6 %all-to-all-start = ((bf16[16,4,1024]{2,1,0:T(4,128)(2,1)}), bf16[16,4,1024]{2,1,0:T(4,128)(2,1)S(1)}, u32[]{:S(2)}, u32[]{:S(2)}) async-start(bf16[16,4,1024]{2,1,0:T(4,128)(2,1)} %param.16), calls=%async_computation | async-start | bytes 262144 | tf_op jit(solution)/shard_map/all_to_all | solution.py:163
  47.4 3.8 %fusion.25 = f32[8,2,4,8,128]{4,3,2,1,0:T(8,128)S(1)} fusion(bf16[8,1024,2,2,128]{1,4,3,2,0:T(8,128)(2,1)} %bitcast.181, f32[8,2,4,8,1024]{4,3,2,1,0:T(8,128)S(1)} %get-tuple-element.228, f32[8,4,2,8]{3,1,2,0:T(4,128)S(1)} %max.18, pred[8,1024]{1,0:T(8,128)(4,1)S(1)} %iota_compare_fusion), kind=kOutput, calls=%fused_computation.44 | convolution fusion | flops 136839168 | bytes 6602752 | tf_op jit(solution)/shard_map/rjhgc,rchd->rjhgd/dot_general | solution.py:211
  53.2 17.9 %all-gather.3.cloned.1.call-done = bf16[8192,256]{1,0:T(8,128)(2,1)} async-done(((bf16[512,256]{1,0:T(8,128)(2,1)}), bf16[8192,256]{1,0:T(8,128)(2,1)}) %all-gather.3.cloned.1.call-update) | async-done | bytes 4194320 | tf_op jit(solution)/shard_map/all_gather | solution.py:116
  71.1 6.9 %reshape.690 = bf16[16,512,1,2,128]{4,3,1,0,2:T(2,128)(2,1)} reshape(bf16[8192,256]{1,0:T(8,128)(2,1)} %all-gather.3.cloned.1.call-done) | data formatting | bytes 8388608 | tf_op jit(solution)/shard_map/reshape | solution.py:120
  78.0 196.6 %while.17 = (s32[]{:T(128)}, f32[256,1,8]{0,2,1:T(8,128)S(1)}, f32[256,1,8]{0,2,1:T(8,128)S(1)}, f32[256,1,8,128]{0,3,2,1:T(8,128)S(1)}, s32[16]{0:T(128)S(1)}, ...) while((s32[]{:T(128)}, f32[256,1,8]{0,2,1:T(8,128)S(1)}, ...), condition=%wide.region_3.4_spmd.clone, body=%wide.region_0.3_spmd.clone.sunk | while | flops 551592704 | bytes 33955008 | solution.py:142
  85.4 3.4 %fusion.80 = f32[256,8]{0,1:T(8,128)S(1)} fusion(f32[512,256,8]{1,0,2:T(8,128)} %get-tuple-element.292, f32[256,8]{0,1:T(8,128)S(1)} %bitcast.184, pred[256,512]{0,1:T(8,128)(4,1)S(1)} %compare_and_fusion.3), kind=kLoop, calls=%fused_computation.6.clone.1 | loop fusion | flops 5240832 | bytes 4341760 | tf_op jit(solution)/shard_map/while/body/eval_jaxpr/reduce_sum | solution.py:100
  97.7 3.3 %fusion.80 = f32[256,8]{0,1:T(8,128)S(1)} fusion(f32[512,256,8]{1,0,2:T(8,128)} %get-tuple-element.292, f32[256,8]{0,1:T(8,128)S(1)} %bitcast.184, pred[256,512]{0,1:T(8,128)(4,1)S(1)} %compare_and_fusion.3), kind=kLoop, calls=%fused_computation.6.clone.1 | loop fusion | flops 5240832 | bytes 4341760 | tf_op jit(solution)/shard_map/while/body/eval_jaxpr/reduce_sum | solution.py:100
  110.0 3.3 %fusion.80 = f32[256,8]{0,1:T(8,128)S(1)} fusion(f32[512,256,8]{1,0,2:T(8,128)} %get-tuple-element.292, f32[256,8]{0,1:T(8,128)S(1)} %bitcast.184, pred[256,512]{0,1:T(8,128)(4,1)S(1)} %compare_and_fusion.3), kind=kLoop, calls=%fused_computation.6.clone.1 | loop fusion | flops 5240832 | bytes 4341760 | tf_op jit(solution)/shard_map/while/body/eval_jaxpr/reduce_sum | solution.py:100
  122.3 3.5 %fusion.80 = f32[256,8]{0,1:T(8,128)S(1)} fusion(f32[512,256,8]{1,0,2:T(8,128)} %get-tuple-element.292, f32[256,8]{0,1:T(8,128)S(1)} %bitcast.184, pred[256,512]{0,1:T(8,128)(4,1)S(1)} %compare_and_fusion.3), kind=kLoop, calls=%fused_computation.6.clone.1 | loop fusion | flops 5240832 | bytes 4341760 | tf_op jit(solution)/shard_map/while/body/eval_jaxpr/reduce_sum | solution.py:100
  134.8 3.3 %fusion.80 = f32[256,8]{0,1:T(8,128)S(1)} fusion(f32[512,256,8]{1,0,2:T(8,128)} %get-tuple-element.292, f32[256,8]{0,1:T(8,128)S(1)} %bitcast.184, pred[256,512]{0,1:T(8,128)(4,1)S(1)} %compare_and_fusion.3), kind=kLoop, calls=%fused_computation.6.clone.1 | loop fusion | flops 5240832 | bytes 4341760 | tf_op jit(solution)/shard_map/while/body/eval_jaxpr/reduce_sum | solution.py:100
  147.1 3.3 %fusion.80 = f32[256,8]{0,1:T(8,128)S(1)} fusion(f32[512,256,8]{1,0,2:T(8,128)} %get-tuple-element.292, f32[256,8]{0,1:T(8,128)S(1)} %bitcast.184, pred[256,512]{0,1:T(8,128)(4,1)S(1)} %compare_and_fusion.3), kind=kLoop, calls=%fused_computation.6.clone.1 | loop fusion | flops 5240832 | bytes 4341760 | tf_op jit(solution)/shard_map/while/body/eval_jaxpr/reduce_sum | solution.py:100
  159.3 3.3 %fusion.80 = f32[256,8]{0,1:T(8,128)S(1)} fusion(f32[512,256,8]{1,0,2:T(8,128)} %get-tuple-element.292, f32[256,8]{0,1:T(8,128)S(1)} %bitcast.184, pred[256,512]{0,1:T(8,128)(4,1)S(1)} %compare_and_fusion.3), kind=kLoop, calls=%fused_computation.6.clone.1 | loop fusion | flops 5240832 | bytes 4341760 | tf_op jit(solution)/shard_map/while/body/eval_jaxpr/reduce_sum | solution.py:100
  171.6 3.3 %fusion.80 = f32[256,8]{0,1:T(8,128)S(1)} fusion(f32[512,256,8]{1,0,2:T(8,128)} %get-tuple-element.292, f32[256,8]{0,1:T(8,128)S(1)} %bitcast.184, pred[256,512]{0,1:T(8,128)(4,1)S(1)} %compare_and_fusion.3), kind=kLoop, calls=%fused_computation.6.clone.1 | loop fusion | flops 5240832 | bytes 4341760 | tf_op jit(solution)/shard_map/while/body/eval_jaxpr/reduce_sum | solution.py:100
  183.9 3.3 %fusion.80 = f32[256,8]{0,1:T(8,128)S(1)} fusion(f32[512,256,8]{1,0,2:T(8,128)} %get-tuple-element.292, f32[256,8]{0,1:T(8,128)S(1)} %bitcast.184, pred[256,512]{0,1:T(8,128)(4,1)S(1)} %compare_and_fusion.3), kind=kLoop, calls=%fused_computation.6.clone.1 | loop fusion | flops 5240832 | bytes 4341760 | tf_op jit(solution)/shard_map/while/body/eval_jaxpr/reduce_sum | solution.py:100
  196.1 3.3 %fusion.80 = f32[256,8]{0,1:T(8,128)S(1)} fusion(f32[512,256,8]{1,0,2:T(8,128)} %get-tuple-element.292, f32[256,8]{0,1:T(8,128)S(1)} %bitcast.184, pred[256,512]{0,1:T(8,128)(4,1)S(1)} %compare_and_fusion.3), kind=kLoop, calls=%fused_computation.6.clone.1 | loop fusion | flops 5240832 | bytes 4341760 | tf_op jit(solution)/shard_map/while/body/eval_jaxpr/reduce_sum | solution.py:100
  208.4 3.3 %fusion.80 = f32[256,8]{0,1:T(8,128)S(1)} fusion(f32[512,256,8]{1,0,2:T(8,128)} %get-tuple-element.292, f32[256,8]{0,1:T(8,128)S(1)} %bitcast.184, pred[256,512]{0,1:T(8,128)(4,1)S(1)} %compare_and_fusion.3), kind=kLoop, calls=%fused_computation.6.clone.1 | loop fusion | flops 5240832 | bytes 4341760 | tf_op jit(solution)/shard_map/while/body/eval_jaxpr/reduce_sum | solution.py:100
  220.7 3.3 %fusion.80 = f32[256,8]{0,1:T(8,128)S(1)} fusion(f32[512,256,8]{1,0,2:T(8,128)} %get-tuple-element.292, f32[256,8]{0,1:T(8,128)S(1)} %bitcast.184, pred[256,512]{0,1:T(8,128)(4,1)S(1)} %compare_and_fusion.3), kind=kLoop, calls=%fused_computation.6.clone.1 | loop fusion | flops 5240832 | bytes 4341760 | tf_op jit(solution)/shard_map/while/body/eval_jaxpr/reduce_sum | solution.py:100
  233.0 3.3 %fusion.80 = f32[256,8]{0,1:T(8,128)S(1)} fusion(f32[512,256,8]{1,0,2:T(8,128)} %get-tuple-element.292, f32[256,8]{0,1:T(8,128)S(1)} %bitcast.184, pred[256,512]{0,1:T(8,128)(4,1)S(1)} %compare_and_fusion.3), kind=kLoop, calls=%fused_computation.6.clone.1 | loop fusion | flops 5240832 | bytes 4341760 | tf_op jit(solution)/shard_map/while/body/eval_jaxpr/reduce_sum | solution.py:100
  245.2 3.3 %fusion.80 = f32[256,8]{0,1:T(8,128)S(1)} fusion(f32[512,256,8]{1,0,2:T(8,128)} %get-tuple-element.292, f32[256,8]{0,1:T(8,128)S(1)} %bitcast.184, pred[256,512]{0,1:T(8,128)(4,1)S(1)} %compare_and_fusion.3), kind=kLoop, calls=%fused_computation.6.clone.1 | loop fusion | flops 5240832 | bytes 4341760 | tf_op jit(solution)/shard_map/while/body/eval_jaxpr/reduce_sum | solution.py:100
  257.5 3.3 %fusion.80 = f32[256,8]{0,1:T(8,128)S(1)} fusion(f32[512,256,8]{1,0,2:T(8,128)} %get-tuple-element.292, f32[256,8]{0,1:T(8,128)S(1)} %bitcast.184, pred[256,512]{0,1:T(8,128)(4,1)S(1)} %compare_and_fusion.3), kind=kLoop, calls=%fused_computation.6.clone.1 | loop fusion | flops 5240832 | bytes 4341760 | tf_op jit(solution)/shard_map/while/body/eval_jaxpr/reduce_sum | solution.py:100
  269.8 3.3 %fusion.80 = f32[256,8]{0,1:T(8,128)S(1)} fusion(f32[512,256,8]{1,0,2:T(8,128)} %get-tuple-element.292, f32[256,8]{0,1:T(8,128)S(1)} %bitcast.184, pred[256,512]{0,1:T(8,128)(4,1)S(1)} %compare_and_fusion.3), kind=kLoop, calls=%fused_computation.6.clone.1 | loop fusion | flops 5240832 | bytes 4341760 | tf_op jit(solution)/shard_map/while/body/eval_jaxpr/reduce_sum | solution.py:100
  275.8 3.6 %gather_fusion = bf16[128,512]{1,0:T(8,128)(2,1)S(1)} fusion(bf16[4096,512]{1,0:T(8,128)(2,1)} %all-gather.5.cloned.1.call-done, s32[1024]{0:T(1024)S(1)} %pad_clamp_fusion), kind=kCustom, calls=%fused_computation | custom fusion | bytes 262656 | tf_op jit(solution)/shard_map/gather | solution.py:40
  (285 shorter events, 164.1 us)
Async XLA Ops:
  7.2 16.7 %copy-start.1 = (bf16[256,1024]{1,0:T(8,128)(2,1)S(1)}, bf16[256,1024]{1,0:T(8,128)(2,1)}, u32[]{:S(2)}) copy-start(bf16[256,1024]{1,0:T(8,128)(2,1)} %param.11) | copy-start | bytes 1572868
  7.2 63.9 %all-gather.3.cloned.1.call-start = ((), (), s32[]{:S(2)}) async-start(), calls=%async_computation.2 | async-start | bytes 4456448 | tf_op jit(solution)/shard_map/all_gather | solution.py:116
  11.9 24.6 %all-to-all-start.1 = ((bf16[16,4,256]{2,1,0:T(4,128)(2,1)}), bf16[16,4,256]{2,1,0:T(4,128)(2,1)S(1)}, u32[]{:S(2)}, u32[]{:S(2)}) async-start(bf16[16,4,256]{2,1,0:T(4,128)(2,1)} %param.17), calls=%async_computation.1 | async-start | bytes 65536 | tf_op jit(solution)/shard_map/all_to_all | solution.py:164
  15.2 260.6 %all-gather.5.cloned.1.call-start = ((), (), s32[]{:S(2)}) async-start(), calls=%async_computation.3 | async-start | bytes 4456448 | tf_op jit(solution)/shard_map/all_gather | solution.py:160
  36.5 6.7 %all-to-all-start = ((bf16[16,4,1024]{2,1,0:T(4,128)(2,1)}), bf16[16,4,1024]{2,1,0:T(4,128)(2,1)S(1)}, u32[]{:S(2)}, u32[]{:S(2)}) async-start(bf16[16,4,1024]{2,1,0:T(4,128)(2,1)} %param.16), calls=%async_computation | async-start | bytes 262144 | tf_op jit(solution)/shard_map/all_to_all | solution.py:163
  85.4 3.5 %copy-start = (f32[512,256,8]{1,0,2:T(8,128)S(1)}, f32[512,256,8]{1,0,2:T(8,128)}, u32[]{:S(2)}) copy-start(f32[512,256,8]{1,0,2:T(8,128)} %get-tuple-element.292) | copy-start | bytes 12582916 | tf_op jit(solution)/shard_map/while
  97.7 3.4 %copy-start = (f32[512,256,8]{1,0,2:T(8,128)S(1)}, f32[512,256,8]{1,0,2:T(8,128)}, u32[]{:S(2)}) copy-start(f32[512,256,8]{1,0,2:T(8,128)} %get-tuple-element.292) | copy-start | bytes 12582916 | tf_op jit(solution)/shard_map/while
  109.9 3.5 %copy-start = (f32[512,256,8]{1,0,2:T(8,128)S(1)}, f32[512,256,8]{1,0,2:T(8,128)}, u32[]{:S(2)}) copy-start(f32[512,256,8]{1,0,2:T(8,128)} %get-tuple-element.292) | copy-start | bytes 12582916 | tf_op jit(solution)/shard_map/while
  122.3 3.7 %copy-start = (f32[512,256,8]{1,0,2:T(8,128)S(1)}, f32[512,256,8]{1,0,2:T(8,128)}, u32[]{:S(2)}) copy-start(f32[512,256,8]{1,0,2:T(8,128)} %get-tuple-element.292) | copy-start | bytes 12582916 | tf_op jit(solution)/shard_map/while
  134.8 3.4 %copy-start = (f32[512,256,8]{1,0,2:T(8,128)S(1)}, f32[512,256,8]{1,0,2:T(8,128)}, u32[]{:S(2)}) copy-start(f32[512,256,8]{1,0,2:T(8,128)} %get-tuple-element.292) | copy-start | bytes 12582916 | tf_op jit(solution)/shard_map/while
  147.1 3.4 %copy-start = (f32[512,256,8]{1,0,2:T(8,128)S(1)}, f32[512,256,8]{1,0,2:T(8,128)}, u32[]{:S(2)}) copy-start(f32[512,256,8]{1,0,2:T(8,128)} %get-tuple-element.292) | copy-start | bytes 12582916 | tf_op jit(solution)/shard_map/while
  159.3 3.4 %copy-start = (f32[512,256,8]{1,0,2:T(8,128)S(1)}, f32[512,256,8]{1,0,2:T(8,128)}, u32[]{:S(2)}) copy-start(f32[512,256,8]{1,0,2:T(8,128)} %get-tuple-element.292) | copy-start | bytes 12582916 | tf_op jit(solution)/shard_map/while
  171.6 3.4 %copy-start = (f32[512,256,8]{1,0,2:T(8,128)S(1)}, f32[512,256,8]{1,0,2:T(8,128)}, u32[]{:S(2)}) copy-start(f32[512,256,8]{1,0,2:T(8,128)} %get-tuple-element.292) | copy-start | bytes 12582916 | tf_op jit(solution)/shard_map/while
  183.9 3.4 %copy-start = (f32[512,256,8]{1,0,2:T(8,128)S(1)}, f32[512,256,8]{1,0,2:T(8,128)}, u32[]{:S(2)}) copy-start(f32[512,256,8]{1,0,2:T(8,128)} %get-tuple-element.292) | copy-start | bytes 12582916 | tf_op jit(solution)/shard_map/while
  196.1 3.4 %copy-start = (f32[512,256,8]{1,0,2:T(8,128)S(1)}, f32[512,256,8]{1,0,2:T(8,128)}, u32[]{:S(2)}) copy-start(f32[512,256,8]{1,0,2:T(8,128)} %get-tuple-element.292) | copy-start | bytes 12582916 | tf_op jit(solution)/shard_map/while
  208.4 3.4 %copy-start = (f32[512,256,8]{1,0,2:T(8,128)S(1)}, f32[512,256,8]{1,0,2:T(8,128)}, u32[]{:S(2)}) copy-start(f32[512,256,8]{1,0,2:T(8,128)} %get-tuple-element.292) | copy-start | bytes 12582916 | tf_op jit(solution)/shard_map/while
  220.7 3.4 %copy-start = (f32[512,256,8]{1,0,2:T(8,128)S(1)}, f32[512,256,8]{1,0,2:T(8,128)}, u32[]{:S(2)}) copy-start(f32[512,256,8]{1,0,2:T(8,128)} %get-tuple-element.292) | copy-start | bytes 12582916 | tf_op jit(solution)/shard_map/while
  232.9 3.4 %copy-start = (f32[512,256,8]{1,0,2:T(8,128)S(1)}, f32[512,256,8]{1,0,2:T(8,128)}, u32[]{:S(2)}) copy-start(f32[512,256,8]{1,0,2:T(8,128)} %get-tuple-element.292) | copy-start | bytes 12582916 | tf_op jit(solution)/shard_map/while
  245.2 3.4 %copy-start = (f32[512,256,8]{1,0,2:T(8,128)S(1)}, f32[512,256,8]{1,0,2:T(8,128)}, u32[]{:S(2)}) copy-start(f32[512,256,8]{1,0,2:T(8,128)} %get-tuple-element.292) | copy-start | bytes 12582916 | tf_op jit(solution)/shard_map/while
  257.5 3.4 %copy-start = (f32[512,256,8]{1,0,2:T(8,128)S(1)}, f32[512,256,8]{1,0,2:T(8,128)}, u32[]{:S(2)}) copy-start(f32[512,256,8]{1,0,2:T(8,128)} %get-tuple-element.292) | copy-start | bytes 12582916 | tf_op jit(solution)/shard_map/while
  269.8 3.4 %copy-start = (f32[512,256,8]{1,0,2:T(8,128)S(1)}, f32[512,256,8]{1,0,2:T(8,128)}, u32[]{:S(2)}) copy-start(f32[512,256,8]{1,0,2:T(8,128)} %get-tuple-element.292) | copy-start | bytes 12582916 | tf_op jit(solution)/shard_map/while
Sparse Core Ops, SparseCore 0:
  12.0 59.0 all-gather.2
  73.6 53.1 all-gather.4
where the time goes:
time: 289 us; the launch traced here: 287 us
  other arithmetic  107 us (37%)
  matrix products  74.8 us (26%)
  local copies, waits for them, and re-layouts  55.2 us (19%)
  waiting for transfers between devices  20.9 us (7%)
  between operations  15 us (5%)
  starting transfers between devices  6.92 us (2%)
  blocking collectives  5.82 us (2%)
    reduce_sum x16, other arithmetic, attend_block(): weight_sum = weight_sum * factor + jnp.sum(weights, -1)  53.6 us
    dot_general x16, matrix products, attend_block(): jnp.einsum('thgd,shd->thgs', rotated_queries, block_keys, preferred_eleme...  43.7 us
    dynamic_slice x48, local copies, waits for them, and re-layouts, on_device(): running, unused = lax.scan(block_step, running, (page_listing, firsts))  28.3 us
    dot_general x16, matrix products, attend_block(): jnp.einsum('thgs,shd->thgd', weights.astype(jnp.bfloat16), block_values,...  23.1 us
    or x16, other arithmetic, block_step(): key_usable = jnp.logical_or(jnp.logical_not(is_prior), key_pos < start_pos)  21 us
    select_n x16, other arithmetic, block_step(): jnp.where(is_prior, owner * prior_count + local_row, start_pos + owner *...  20.9 us
    all_gather x1, waiting for transfers between devices, on_device(): shard_rows = lax.all_gather(context, 'ctx', axis=0, tiled=True)  17.9 us
    unnamed x8, local copies, waits for them, and re-layouts  12.8 us
  transfers between devices with their start and end apart: 4, of which 2 were waited for; matrix products, arithmetic and copies ran while one was open for 79% of the time, Pallas kernels for 0%

commit v1 on v0

v1 whole, which is shorter than its diff:
```python
import functools
import math

import jax
import jax.numpy as jnp
import numpy as np
from jax import lax
from jax.experimental import pallas as pl
from jax.experimental.pallas import tpu as pltpu
from jax.sharding import PartitionSpec as P

HEAD = 128
GROUP = 8
PAGE = 64
TOK = 256
CHIP = 4 * TOK
ROWS = 8
STEPS = 4
SLOTS = 1024
BLOCK = 512
NEG = -1e30
FAR = 1 << 30
SCALE = math.log2(math.e) / math.sqrt(HEAD)
THETA = 500000.0
MESH = pl.DeviceIdType.MESH
NT = (((1,), (1,)), ((), ()))


def mm(a, b):
    return jnp.dot(a, b, preferred_element_type=jnp.float32)


def mm_nt(a, b):
    return lax.dot_general(a, b, NT, preferred_element_type=jnp.float32)


def rotate(x, cosine, sine):
    return x * cosine + pltpu.roll(x, 64, 1) * sine


def kernel(
    sq_hbm, skv_hbm, ekv_hbm, start_ref, page_ref, dq_hbm, dkv_hbm, cache_hbm, len_ref,
    cos_ref, sin_ref, freq_ref,
    fill_ref, pages_ref, step_ref,
    near_keys, far_keys, sq, skv, qs, acc, top, bias, scores, dq, dkv, cache, qd, od, d_top, d_total, d_acc,
    page_out, page_in,
    load_sem, cache_sem, c_send, c_recv, s_send, s_recv,
    d_send, d_recv, p_send, p_recv,
):
    ctx = lax.axis_index("ctx")
    sec = lax.axis_index("section")
    core = ctx % 2
    z = (ctx // 2) % 4
    x = ctx // 8
    sibling = {"ctx": x * 8 + z * 2 + 1 - core}
    partner = {"section": 1 - sec}
    start = start_ref[0]

    def chip_of(dx, dz):
        column = x if dx == 0 else 1 - x
        return column * 4 + (z + dz) % 4

    near = ((0, 0), (1, 0), (0, 1), (0, 3))
    far = ((1, 1), (1, 3), (0, 2), (1, 2))

    def place(dx, dz, piece, other_core=0):
        ref, ways = (near_keys, near) if (dx, dz) in near else (far_keys, far)
        return ref.at[pl.ds(ways.index((dx, dz)) * CHIP + (2 * piece + other_core) * TOK, TOK)]

    def remote(src, dst, send, recv, device):
        return pltpu.make_async_remote_copy(
            src_ref=src, dst_ref=dst, send_sem=send, recv_sem=recv,
            device_id=device, device_id_type=MESH,
        )

    def peer(dx, dz):
        return {"ctx": chip_of(dx, dz) * 2 + core}

    def chip_copy(piece, dx, dz):
        back = (4 - dz) % 4
        return remote(
            place(0, 0, piece), place(dx, back, piece),
            c_send.at[piece, dx, dz], c_recv.at[piece, dx, back], peer(dx, dz),
        )

    def chip_arrival(piece, dx, dz):
        ref = place(dx, dz, piece)
        return remote(ref, ref, c_send.at[piece, dx, dz], c_recv.at[piece, dx, dz], peer(dx, dz))

    def core_copy(piece, dx, dz):
        return remote(
            place(dx, dz, piece), place(dx, dz, piece, 1),
            s_send.at[piece, dx, dz], s_recv.at[piece, dx, dz], sibling,
        )

    def pass_on(ways):
        for dx, dz in ways:
            for piece in (0, 1):
                chip_arrival(piece, dx, dz).wait_recv()
                core_copy(piece, dx, dz).start()

    def from_sibling(ways):
        for dx, dz in ways:
            for piece in (0, 1):
                core_copy(piece, dx, dz).wait_recv()

    barrier = pltpu.get_barrier_semaphore()
    for device in [peer(dx, dz) for dx, dz in near[1:] + far] + [sibling, partner]:
        pl.semaphore_signal(barrier, inc=1, device_id=device, device_id_type=MESH)

    load_e = pltpu.make_async_copy(ekv_hbm, place(0, 0, 0), load_sem.at[0])
    load_kv = pltpu.make_async_copy(skv_hbm, skv, load_sem.at[1])
    load_q = pltpu.make_async_copy(sq_hbm, sq, load_sem.at[2])
    load_e.start()
    load_kv.start()
    load_q.start()
    mine = pl.ds(sec * ROWS, ROWS)
    other = pl.ds((1 - sec) * ROWS, ROWS)
    load_dq = pltpu.make_async_copy(dq_hbm.at[mine], dq.at[sec], load_sem.at[3])
    load_dkv = pltpu.make_async_copy(dkv_hbm.at[mine], dkv.at[sec], load_sem.at[4])
    load_dq.start()
    load_dkv.start()

    def cache_copy(row):
        return pltpu.make_async_copy(cache_hbm.at[row], cache.at[row], cache_sem.at[row])

    for row in range(ROWS):
        cache_copy(row).start()

    lane = lax.broadcasted_iota(jnp.int32, (1, HEAD), 1)
    sign = jnp.where(lane < HEAD // 2, -1.0, 1.0)
    freq = freq_ref[0:1, :]
    first_angle = (start + ctx * TOK).astype(jnp.float32) * freq_ref[...]
    base_cos = jnp.cos(first_angle)[0:1]
    base_sin = jnp.sin(first_angle)[0:1]
    cosine = cos_ref[...] * base_cos - sin_ref[...] * base_sin
    sine = (sin_ref[...] * base_cos + cos_ref[...] * base_sin) * sign

    load_kv.wait()
    turned = rotate(skv[:, :HEAD].astype(jnp.float32), cosine, sine).astype(jnp.bfloat16)
    fresh_rows = slice(2 * TOK, 3 * TOK)
    near_keys[fresh_rows, :HEAD] = turned
    near_keys[fresh_rows, HEAD:] = skv[:, HEAD:]

    load_e.wait()
    pl.semaphore_wait(barrier, 9)
    send_dq = remote(dq_hbm.at[other], dq.at[sec], d_send.at[0], d_recv.at[0], partner)
    send_dkv = remote(dkv_hbm.at[other], dkv.at[sec], d_send.at[1], d_recv.at[1], partner)
    for piece in (0, 1):
        for dx, dz in near[1:]:
            chip_copy(piece, dx, dz).start()
        core_copy(piece, 0, 0).start()
        if piece == 0:
            send_dkv.start()
            send_dq.start()

    load_q.wait()
    for g in range(GROUP):
        part = sq[:, g * HEAD : (g + 1) * HEAD].astype(jnp.float32)
        scaled = rotate(part, cosine, sine).astype(jnp.bfloat16).astype(jnp.float32) * SCALE
        high = scaled.astype(jnp.bfloat16)
        low = (scaled - high.astype(jnp.float32)).astype(jnp.bfloat16)
        qs[g * TOK : (g + 1) * TOK, :] = jnp.concatenate([high, low], 1)

    load_dq.wait()
    load_dkv.wait()
    remote(dkv_hbm.at[other], dkv.at[1 - sec], d_send.at[1], d_recv.at[1], partner).wait_recv()
    remote(dq_hbm.at[other], dq.at[1 - sec], d_send.at[0], d_recv.at[0], partner).wait_recv()
    line = lax.broadcasted_iota(jnp.int32, (ROWS * STEPS, HEAD), 0)
    position = line % STEPS
    for row in range(ROWS):
        position = position + jnp.where(line // STEPS == row, len_ref[row], 0)
    angle = position.astype(jnp.float32) * freq
    step_cos = jnp.cos(angle)
    step_sin = jnp.sin(angle) * sign
    count = ROWS * STEPS * GROUP
    to_line = lax.broadcasted_iota(jnp.int32, (count, count), 0)
    from_line = lax.broadcasted_iota(jnp.int32, (count, count), 1)
    per_row = STEPS * GROUP
    wanted = (
        (to_line // STEPS) % GROUP * (ROWS * STEPS)
        + to_line // per_row * STEPS
        + to_line % STEPS
    )
    permute = jnp.where(wanted == from_line, 1.0, 0.0).astype(jnp.bfloat16)
    q_line = lax.broadcasted_iota(jnp.int32, (count, ROWS * STEPS), 0)
    k_line = lax.broadcasted_iota(jnp.int32, (count, ROWS * STEPS), 1)
    fresh_ok = (q_line // per_row == k_line // STEPS) & (k_line % STEPS <= q_line % STEPS)
    slot = lax.broadcasted_iota(jnp.int32, (1, SLOTS), 1)
    for h in range(2):
        lines = dq[h].astype(jnp.float32).reshape(ROWS * STEPS, GROUP * HEAD)
        parts = [
            rotate(lines[:, g * HEAD : (g + 1) * HEAD], step_cos, step_sin)
            for g in range(GROUP)
        ]
        ordered = mm(permute, jnp.concatenate(parts, 0).astype(jnp.bfloat16))
        ordered = ordered.astype(jnp.bfloat16)
        qd[h] = ordered
        fresh = dkv[h].astype(jnp.float32).reshape(ROWS * STEPS, 2 * HEAD)
        step_key = rotate(fresh[:, :HEAD], step_cos, step_sin).astype(jnp.bfloat16)
        s = jnp.where(fresh_ok, mm_nt(ordered, step_key) * SCALE, NEG)
        m = jnp.max(s, -1, keepdims=True)
        p = jnp.exp2(s - m)
        d_top[h] = m
        d_total[h] = jnp.sum(p, -1, keepdims=True)
        d_acc[h] = mm(p.astype(jnp.bfloat16), fresh[:, HEAD:].astype(jnp.bfloat16))

    def decode_row(row, carry):
        mask = slot < len_ref[row]
        lines = pl.ds(pl.multiple_of(row * per_row, per_row), per_row)
        for h in range(2):
            m0, l0, a0 = d_top[h, lines, :], d_total[h, lines, :], d_acc[h, lines, :]
            s = mm_nt(qd[h, lines, :], cache[row, :, h * 256 : h * 256 + 128])
            s = jnp.where(mask, s * SCALE, NEG)
            m = jnp.maximum(m0, jnp.max(s, -1, keepdims=True))
            p = jnp.exp2(s - m)
            factor = jnp.exp2(m0 - m)
            weight = l0 * factor + jnp.sum(p, -1, keepdims=True)
            mixed = a0 * factor + mm(
                p.astype(jnp.bfloat16), cache[row, :, h * 256 + 128 : (h + 1) * 256]
            )
            od[h, lines, :] = (mixed / weight).astype(jnp.bfloat16)
        return carry

    for row in range(ROWS):
        cache_copy(row).wait()
    lax.fori_loop(0, ROWS // 2, decode_row, 0)
    for piece in (0, 1):
        for dx, dz in far:
            chip_copy(piece, dx, dz).start()
    pass_on(near[1:])
    lax.fori_loop(ROWS // 2, ROWS, decode_row, 0)
    for h in range(2):
        back = lax.dot_general(
            permute, od[h], (((0,), (0,)), ((), ())), preferred_element_type=jnp.float32
        )
        for g in range(GROUP):
            lines = back[g * ROWS * STEPS : (g + 1) * ROWS * STEPS]
            lanes = slice((h * GROUP + g) * HEAD, (h * GROUP + g + 1) * HEAD)
            step_ref[:, :, lanes] = lines.reshape(ROWS, STEPS, HEAD).astype(jnp.bfloat16)

    key_lane = lax.broadcasted_iota(jnp.int32, (1, CHIP), 1)
    in_core = key_lane % (2 * TOK) // TOK
    in_chip = (core + in_core - 2 * core * in_core) * TOK + key_lane % TOK
    own_chip = chip_of(0, 0)
    for i, way in enumerate(near + far):
        chip = chip_of(*way)
        earlier = jnp.where(chip * 2 * TOK + in_chip < start, 0.0, NEG)
        fresh = jnp.where(own_chip >= chip, 0.0, NEG)
        bias[i : i + 1, :] = jnp.where(key_lane < 2 * TOK, earlier, fresh)
    own_limit = jnp.where(key_lane < 2 * TOK, -1, own_chip * 2 * TOK + in_chip)
    token = ctx * TOK + lax.broadcasted_iota(jnp.int32, (BLOCK, 1), 0) % TOK
    ones = jnp.ones((CHIP, HEAD), jnp.bfloat16)
    blocks = GROUP * TOK // BLOCK

    def lines_of(block):
        return pl.ds(pl.multiple_of(block * BLOCK, BLOCK), BLOCK)

    def score(block, part, i):
        key = (near_keys, far_keys)[part][i * CHIP : (i + 1) * CHIP, :HEAD]
        s = mm_nt(qs[lines_of(block), :], jnp.concatenate([key, key], 1))
        s = s + bias[part * 4 + i : part * 4 + i + 1, :]
        return jnp.where(own_limit <= token, s, NEG) if part == 0 and i == 0 else s

    def step(part, block, carry):
        lines = lines_of(block)
        m, a = top[lines, :], acc[lines, :]
        s = scores[...]
        for i in range(4):
            if i < 3:
                following = score(block, part, i + 1)
            else:
                scores[...] = score((block + 1) % blocks, part, 0)
            higher = jnp.maximum(m, jnp.max(s, -1, keepdims=True))
            p = jnp.exp2(s - higher)
            values = (near_keys, far_keys)[part][i * CHIP : (i + 1) * CHIP, HEAD:]
            a = a * jnp.exp2(m - higher) + mm(
                p.astype(jnp.bfloat16), jnp.concatenate([values, ones], 1)
            )
            m = higher
            s = following
        top[lines, :], acc[lines, :] = m, a
        return carry

    from_sibling(near)
    acc[...] = jnp.zeros_like(acc)
    top[...] = jnp.full_like(top, NEG)
    scores[...] = score(0, 0, 0)
    lax.fori_loop(0, blocks, functools.partial(step, 0), 0)

    pass_on(far)
    from_sibling(far)

    own_page = (ctx * 2 + sec) * 2
    other_page = (ctx * 2 + 1 - sec) * 2
    wanted_pages = (own_page, own_page + 1, other_page, other_page + 1)

    def seek(block, found):
        page = page_ref[block]
        return tuple(
            jnp.where(page == wanted, block, old) for wanted, old in zip(wanted_pages, found)
        )

    found = lax.fori_loop(0, page_ref.shape[0], seek, (jnp.int32(0),) * 4)

    pick = lax.broadcasted_iota(jnp.int32, (4 * PAGE, 1), 0)
    source = pick % PAGE
    for i in range(4):
        source = source + jnp.where(pick // PAGE == i, found[i] * PAGE, 0)
    picked = jnp.zeros((4 * PAGE, 2 * HEAD), jnp.float32)
    for i, way in enumerate(near + far):
        held = chip_of(*way) * 2 * TOK + in_chip[:, : 2 * TOK]
        chosen = jnp.where(source == held, 1.0, 0.0).astype(jnp.bfloat16)
        rows = slice(i % 4 * CHIP + 2 * TOK, (i % 4 + 1) * CHIP)
        picked = picked + mm(chosen, (near_keys, far_keys)[i // 4][rows, :])
    picked = picked.astype(jnp.bfloat16).reshape(4, PAGE, 2 * HEAD)
    page_out[...] = picked[2:]
    page_copy = remote(page_out, page_in, p_send, p_recv, partner)
    page_copy.start()
    width = 2 * HEAD
    pages_ref[:, :, pl.ds(pl.multiple_of(sec * width, width), width)] = picked[:2]

    scores[...] = score(0, 1, 0)
    lax.fori_loop(0, blocks, functools.partial(step, 1), 0)
    for g in range(GROUP):
        a = acc[g * TOK : (g + 1) * TOK, :]
        fill_ref[:, g * HEAD : (g + 1) * HEAD] = (a[:, :HEAD] / a[:, HEAD:]).astype(jnp.bfloat16)

    page_copy.wait_recv()
    pages_ref[:, :, pl.ds(pl.multiple_of((1 - sec) * width, width), width)] = page_in[...]

    page_copy.wait_send()
    send_dq.wait_send()
    send_dkv.wait_send()
    for piece in (0, 1):
        for dx, dz in near[1:] + far:
            chip_copy(piece, dx, dz).wait_send()
        for dx, dz in near + far:
            core_copy(piece, dx, dz).wait_send()


def on_device(*args):
    offset = np.arange(TOK)[:, None]
    half = THETA ** (-np.arange(HEAD // 2) * 2.0 / HEAD)
    freq = np.concatenate([half, half]).astype(np.float32)
    angles = offset * freq.astype(np.float64)[None, :]
    any_spec = pl.BlockSpec(memory_space=pl.ANY)
    smem = pl.BlockSpec(memory_space=pltpu.SMEM)
    vmem = pl.BlockSpec(memory_space=pltpu.VMEM)
    bf16 = jnp.bfloat16
    dma = pltpu.SemaphoreType.DMA
    return pl.pallas_call(
        kernel,
        out_shape=(
            jax.ShapeDtypeStruct((TOK, GROUP * HEAD), bf16),
            jax.ShapeDtypeStruct((2, PAGE, 4 * HEAD), bf16),
            jax.ShapeDtypeStruct((ROWS, STEPS, 2 * GROUP * HEAD), bf16),
        ),
        in_specs=[any_spec, any_spec, any_spec, smem, smem, any_spec, any_spec, any_spec, smem]
        + [vmem] * 3,
        out_specs=(vmem,) * 3,
        scratch_shapes=[
            pltpu.VMEM((4 * CHIP, 2 * HEAD), bf16),
            pltpu.VMEM((4 * CHIP, 2 * HEAD), bf16),
            pltpu.VMEM((TOK, GROUP * HEAD), bf16),
            pltpu.VMEM((TOK, 2 * HEAD), bf16),
            pltpu.VMEM((GROUP * TOK, 2 * HEAD), bf16),
            pltpu.VMEM((GROUP * TOK, 2 * HEAD), jnp.float32),
            pltpu.VMEM((GROUP * TOK, 1), jnp.float32),
            pltpu.VMEM((8, CHIP), jnp.float32),
            pltpu.VMEM((BLOCK, CHIP), jnp.float32),
            pltpu.VMEM((2, ROWS, STEPS, GROUP * HEAD), bf16),
            pltpu.VMEM((2, ROWS, STEPS, 2 * HEAD), bf16),
            pltpu.VMEM((ROWS, SLOTS, 4 * HEAD), bf16),
            pltpu.VMEM((2, ROWS * STEPS * GROUP, HEAD), bf16),
            pltpu.VMEM((2, ROWS * STEPS * GROUP, HEAD), bf16),
            pltpu.VMEM((2, ROWS * STEPS * GROUP, 1), jnp.float32),
            pltpu.VMEM((2, ROWS * STEPS * GROUP, 1), jnp.float32),
            pltpu.VMEM((2, ROWS * STEPS * GROUP, HEAD), jnp.float32),
            pltpu.VMEM((2, PAGE, 2 * HEAD), bf16),
            pltpu.VMEM((2, PAGE, 2 * HEAD), bf16),
            dma((5,)),
            dma((ROWS,)),
            dma((2, 2, 4)),
            dma((2, 2, 4)),
            dma((2, 2, 4)),
            dma((2, 2, 4)),
            dma((2,)),
            dma((2,)),
            dma,
            dma,
        ],
        compiler_params=pltpu.CompilerParams(
            collective_id=0, has_side_effects=True, vmem_limit_bytes=58 * 2**20
        ),
        cost_estimate=pl.CostEstimate(
            flops=10 * 2**30, bytes_accessed=10 * 2**20, transcendentals=2**24
        ),
    )(
        *args,
        jnp.asarray(np.cos(angles).astype(np.float32)),
        jnp.asarray(np.sin(angles).astype(np.float32)),
        jnp.asarray(np.tile(freq[None, :], (8, 1))),
    )


def solution(mesh):
    in_specs = (
        P("ctx", ("tensor", "section")),
        P("ctx", ("tensor", "section")),
        P("ctx", ("tensor", "section")),
        P(),
        P(),
        P("ctx", None, ("tensor", "section")),
        P("ctx", None, ("tensor", "section")),
        P(("ctx", "section"), None, "tensor"),
        P(("ctx", "section")),
    )
    out_specs = (
        P("ctx", ("tensor", "section")),
        P(("ctx", "section"), None, "tensor"),
        P(("ctx", "section"), None, "tensor"),
    )
    return jax.shard_map(
        on_device, mesh=mesh, in_specs=in_specs, out_specs=out_specs, check_vma=False
    )
```

time: 289 us -> 62.7 us (0.22)
  other arithmetic: 107 us -> 0 us
  matrix products: 74.8 us -> 0 us
  Pallas kernels: 0 us -> 56.1 us
  local copies, waits for them, and re-layouts: 55.2 us -> 5.04 us
  waiting for transfers between devices: 20.9 us -> 0 us
  between operations: 15 us -> 1.29 us
  starting transfers between devices: 6.92 us -> 0 us
  blocking collectives: 5.82 us -> 0 us
    dot_general x36 -> x0, matrix products: 74.8 us -> none  [the longest x16 43.7 us: attend_block(): jnp.einsum('thgd,shd->thgs', rotated_queries, block_keys, preferred_eleme...]
    pallas_call x0 -> x1, Pallas kernels: none -> 56.1 us  [on_device(): pl.pallas_call(kernel, out_shape=(jax.ShapeDtypeStruct((TOK, GROUP * HEAD...]
    reduce_sum x19 -> x0, other arithmetic: 55.3 us -> none  [the longest x16 53.6 us: attend_block(): weight_sum = weight_sum * factor + jnp.sum(weights, -1)]
    dynamic_slice x48 -> x0, local copies, waits for them, and re-layouts: 28.3 us -> none  [on_device(): running, unused = lax.scan(block_step, running, (page_listing, firsts))]
    select_n x18 -> x0, other arithmetic: 21.7 us -> none  [the longest x16 20.9 us: block_step(): jnp.where(is_prior, owner * prior_count + local_row, start_pos + owner *...]
    or x16 -> x0, other arithmetic: 21 us -> none  [block_step(): key_usable = jnp.logical_or(jnp.logical_not(is_prior), key_pos < start_pos)]
    all_gather x2 -> x0, waiting for transfers between devices: 17.9 us -> none  [the longest x1 17.9 us: on_device(): shard_rows = lax.all_gather(context, 'ctx', axis=0, tiled=True)]
    reshape x3 -> x0, local copies, waits for them, and re-layouts: 7.9 us -> none  [the longest x1 6.9 us: on_device(): shard_rows.reshape(block_count, block_rows, local_heads, 2, HEAD_SIZE)]
  transfers between devices with their start and end apart: 4 -> 0, of which waited for: 2 -> 0; matrix products, arithmetic and copies ran while one was open for 79% -> 0% of each run, Pallas kernels for 0% -> 0%
where the time goes in v1:
time: 62.7 us; the launch traced here: 62.5 us
  Pallas kernels  56.1 us (89%)
  local copies, waits for them, and re-layouts  5.04 us (8%)
  between operations  1.29 us (2%)
    pallas_call x1, Pallas kernels, on_device(): pl.pallas_call(kernel, out_shape=(jax.ShapeDtypeStruct((TOK, GROUP * HEAD...  56.1 us
    unnamed x3, local copies, waits for them, and re-layouts  5.04 us

profile of v1, /device:TPU:1, one launch (start us, length us, event | category | flops | bytes accessed | tf_op | source)
XLA Modules:
  0.0 62.5 jit_solution(1912761810162765662)
XLA Ops:
  1.3 56.1 %shard_map.139 = (bf16[256,1024]{1,0:T(8,128)(2,1)}, bf16[2,64,512]{2,1,0:T(8,128)(2,1)}, bf16[8,4,2048]{2,1,0:T(4,128)(2,1)}) custom-call(bf16[256,1024]{1,0:T(8,128)(2,1)} %sq_hbm.1, bf16[256,256]{1,0:T(8,128)(2,1)} %skv_hbm.1, bf16[256,256]{1,0:T(8,128)(2,1)} %ekv_hbm.1, s32[1]{0:T(128)S(6)} %copy.18.start_ref, s32[64]{0:T(128)} %page_ref.1, ...), custom_call_target="tpu_custom_call" | custom-call | flops 10737418240 | bytes 10485760 | tf_op jit(solution)/shard_map/pallas_call | solution.py:352
  57.4 1.9 %copy.19 = bf16[256,1024]{1,0:T(8,128)(2,1)} copy(bf16[256,1024]{1,0:T(8,128)(2,1)} %get-tuple-element.6) | data formatting | bytes 1048576
  59.3 1.6 %copy.20 = bf16[2,64,512]{2,1,0:T(8,128)(2,1)} copy(bf16[2,64,512]{2,1,0:T(8,128)(2,1)} %get-tuple-element.7) | data formatting | bytes 262144
  60.9 1.6 %copy.21 = bf16[8,4,2048]{2,1,0:T(4,128)(2,1)} copy(bf16[8,4,2048]{2,1,0:T(4,128)(2,1)} %get-tuple-element.8) | data formatting | bytes 262144

commit v2 on v1

--- a/solution.py
+++ b/solution.py
@@ -1,4 +1,3 @@
-import functools
 import math
 
 import jax
@@ -61,7 +60,7 @@
         return column * 4 + (z + dz) % 4
 
     near = ((0, 0), (1, 0), (0, 1), (0, 3))
-    far = ((1, 1), (1, 3), (0, 2), (1, 2))
+    far = ((0, 2), (1, 1), (1, 3), (1, 2))
 
     def place(dx, dz, piece, other_core=0):
         ref, ways = (near_keys, near) if (dx, dz) in near else (far_keys, far)
@@ -83,6 +82,13 @@
             c_send.at[piece, dx, dz], c_recv.at[piece, dx, back], peer(dx, dz),
         )
 
+    def onward_copy(piece, dx, dz):
+        source, target = ((0, 2), (1, 2)) if dx else ((1, 0), (1, (4 - dz) % 4))
+        return remote(
+            place(*source, piece), place(*target, piece),
+            c_send.at[piece, 1, dz], c_recv.at[piece, 1, target[1]], peer(dx, 0 if dx else dz),
+        )
+
     def chip_arrival(piece, dx, dz):
         ref = place(dx, dz, piece)
         return remote(ref, ref, c_send.at[piece, dx, dz], c_recv.at[piece, dx, dz], peer(dx, dz))
@@ -105,7 +111,9 @@
                 core_copy(piece, dx, dz).wait_recv()
 
     barrier = pltpu.get_barrier_semaphore()
-    for device in [peer(dx, dz) for dx, dz in near[1:] + far] + [sibling, partner]:
+    direct = near[1:] + far[:1]
+    passed = ((0, 1), (0, 3), (1, 2))
+    for device in [peer(dx, dz) for dx, dz in direct] + [sibling, partner]:
         pl.semaphore_signal(barrier, inc=1, device_id=device, device_id_type=MESH)
 
     load_e = pltpu.make_async_copy(ekv_hbm, place(0, 0, 0), load_sem.at[0])
@@ -143,16 +151,17 @@
     near_keys[fresh_rows, HEAD:] = skv[:, HEAD:]
 
     load_e.wait()
-    pl.semaphore_wait(barrier, 9)
+    pl.semaphore_wait(barrier, 6)
     send_dq = remote(dq_hbm.at[other], dq.at[sec], d_send.at[0], d_recv.at[0], partner)
     send_dkv = remote(dkv_hbm.at[other], dkv.at[sec], d_send.at[1], d_recv.at[1], partner)
+    send_dkv.start()
+    send_dq.start()
     for piece in (0, 1):
         for dx, dz in near[1:]:
             chip_copy(piece, dx, dz).start()
         core_copy(piece, 0, 0).start()
-        if piece == 0:
-            send_dkv.start()
-            send_dq.start()
+    for piece in (0, 1):
+        chip_copy(piece, 0, 2).start()
 
     load_q.wait()
     for g in range(GROUP):
@@ -205,31 +214,35 @@
         d_total[h] = jnp.sum(p, -1, keepdims=True)
         d_acc[h] = mm(p.astype(jnp.bfloat16), fresh[:, HEAD:].astype(jnp.bfloat16))
 
-    def decode_row(row, carry):
-        mask = slot < len_ref[row]
-        lines = pl.ds(pl.multiple_of(row * per_row, per_row), per_row)
-        for h in range(2):
-            m0, l0, a0 = d_top[h, lines, :], d_total[h, lines, :], d_acc[h, lines, :]
-            s = mm_nt(qd[h, lines, :], cache[row, :, h * 256 : h * 256 + 128])
-            s = jnp.where(mask, s * SCALE, NEG)
+    def decode_rows(n, carry):
+        pairs = []
+        for i in range(2):
+            row = 2 * n + i
+            lines = pl.ds(pl.multiple_of(row * per_row, per_row), per_row)
+            for h in range(2):
+                s = mm_nt(qd[h, lines, :], cache[row, :, h * 256 : h * 256 + 128])
+                pairs.append((row, h, lines, s))
+        weights = []
+        for row, h, lines, s in pairs:
+            s = jnp.where(slot < len_ref[row], s * SCALE, NEG)
+            m0 = d_top[h, lines, :]
             m = jnp.maximum(m0, jnp.max(s, -1, keepdims=True))
             p = jnp.exp2(s - m)
             factor = jnp.exp2(m0 - m)
-            weight = l0 * factor + jnp.sum(p, -1, keepdims=True)
-            mixed = a0 * factor + mm(
-                p.astype(jnp.bfloat16), cache[row, :, h * 256 + 128 : (h + 1) * 256]
-            )
-            od[h, lines, :] = (mixed / weight).astype(jnp.bfloat16)
+            total = d_total[h, lines, :] * factor + jnp.sum(p, -1, keepdims=True)
+            weights.append((p.astype(jnp.bfloat16), factor, total))
+        for (row, h, lines, _), (p, factor, total) in zip(pairs, weights):
+            mixed = d_acc[h, lines, :] * factor + mm(p, cache[row, :, h * 256 + 128 : (h + 1) * 256])
+            od[h, lines, :] = (mixed / total).astype(jnp.bfloat16)
         return carry
 
     for row in range(ROWS):
         cache_copy(row).wait()
-    lax.fori_loop(0, ROWS // 2, decode_row, 0)
+    lax.fori_loop(0, ROWS // 2, decode_rows, 0)
+    pass_on(((1, 0),))
     for piece in (0, 1):
-        for dx, dz in far:
-            chip_copy(piece, dx, dz).start()
-    pass_on(near[1:])
-    lax.fori_loop(ROWS // 2, ROWS, decode_row, 0)
+        for dz in (1, 3):
+            onward_copy(piece, 0, dz).start()
     for h in range(2):
         back = lax.dot_general(
             permute, od[h], (((0,), (0,)), ((), ())), preferred_element_type=jnp.float32
@@ -249,47 +262,67 @@
         fresh = jnp.where(own_chip >= chip, 0.0, NEG)
         bias[i : i + 1, :] = jnp.where(key_lane < 2 * TOK, earlier, fresh)
     own_limit = jnp.where(key_lane < 2 * TOK, -1, own_chip * 2 * TOK + in_chip)
-    token = ctx * TOK + lax.broadcasted_iota(jnp.int32, (BLOCK, 1), 0) % TOK
+    token = ctx * TOK + lax.broadcasted_iota(jnp.int32, (2 * BLOCK, 1), 0) % TOK
     ones = jnp.ones((CHIP, HEAD), jnp.bfloat16)
-    blocks = GROUP * TOK // BLOCK
-
-    def lines_of(block):
-        return pl.ds(pl.multiple_of(block * BLOCK, BLOCK), BLOCK)
-
-    def score(block, part, i):
-        key = (near_keys, far_keys)[part][i * CHIP : (i + 1) * CHIP, :HEAD]
-        s = mm_nt(qs[lines_of(block), :], jnp.concatenate([key, key], 1))
-        s = s + bias[part * 4 + i : part * 4 + i + 1, :]
-        return jnp.where(own_limit <= token, s, NEG) if part == 0 and i == 0 else s
-
-    def step(part, block, carry):
-        lines = lines_of(block)
-        m, a = top[lines, :], acc[lines, :]
-        s = scores[...]
-        for i in range(4):
-            if i < 3:
-                following = score(block, part, i + 1)
-            else:
-                scores[...] = score((block + 1) % blocks, part, 0)
-            higher = jnp.maximum(m, jnp.max(s, -1, keepdims=True))
-            p = jnp.exp2(s - higher)
-            values = (near_keys, far_keys)[part][i * CHIP : (i + 1) * CHIP, HEAD:]
-            a = a * jnp.exp2(m - higher) + mm(
-                p.astype(jnp.bfloat16), jnp.concatenate([values, ones], 1)
-            )
-            m = higher
-            s = following
-        top[lines, :], acc[lines, :] = m, a
-        return carry
-
-    from_sibling(near)
+
+    def rows_of(i):
+        return (near_keys, far_keys)[i // 4], slice(i % 4 * CHIP, (i % 4 + 1) * CHIP)
+
+    def attend(chips, size, event=None):
+        blocks = GROUP * TOK // size
+
+        def lines_of(block):
+            return pl.ds(pl.multiple_of(block * size, size), size)
+
+        def score(block, i):
+            ref, rows = rows_of(i)
+            key = ref[rows, :HEAD]
+            s = mm_nt(qs[lines_of(block), :], jnp.concatenate([key, key], 1)) + bias[i : i + 1, :]
+            return jnp.where(own_limit <= token[:size], s, NEG) if i == 0 else s
+
+        def step(block, carry):
+            if event is not None:
+                pl.when(block == 2)(event)
+            lines = lines_of(block)
+            m, a = top[lines, :], acc[lines, :]
+            s = scores[:size, :]
+            for i in chips:
+                if i != chips[-1]:
+                    following = score(block, i + 1)
+                else:
+                    scores[:size, :] = score((block + 1) % blocks, chips[0])
+                higher = jnp.maximum(m, jnp.max(s, -1, keepdims=True))
+                p = jnp.exp2(s - higher)
+                ref, rows = rows_of(i)
+                a = a * jnp.exp2(m - higher) + mm(
+                    p.astype(jnp.bfloat16), jnp.concatenate([ref[rows, HEAD:], ones], 1)
+                )
+                m = higher
+                s = following if i != chips[-1] else None
+            top[lines, :], acc[lines, :] = m, a
+            return carry
+
+        scores[:size, :] = score(0, chips[0])
+        lax.fori_loop(0, blocks, step, 0)
+
     acc[...] = jnp.zeros_like(acc)
     top[...] = jnp.full_like(top, NEG)
-    scores[...] = score(0, 0, 0)
-    lax.fori_loop(0, blocks, functools.partial(step, 0), 0)
-
-    pass_on(far)
-    from_sibling(far)
+    from_sibling(near[:1])
+    attend((0,), 2 * BLOCK)
+    pass_on(near[2:])
+    from_sibling(near[1:])
+
+    def send_across():
+        pass_on(far[:1])
+        for piece in (0, 1):
+            onward_copy(piece, 1, 2).start()
+
+    attend((1, 2, 3), BLOCK, send_across)
+    pass_on(far[1:3])
+    from_sibling(far[:3])
+    attend((4, 5, 6), BLOCK)
+    pass_on(far[3:])
+    from_sibling(far[3:])
 
     own_page = (ctx * 2 + sec) * 2
     other_page = (ctx * 2 + 1 - sec) * 2
@@ -320,8 +353,7 @@
     width = 2 * HEAD
     pages_ref[:, :, pl.ds(pl.multiple_of(sec * width, width), width)] = picked[:2]
 
-    scores[...] = score(0, 1, 0)
-    lax.fori_loop(0, blocks, functools.partial(step, 1), 0)
+    attend((7,), 2 * BLOCK)
     for g in range(GROUP):
         a = acc[g * TOK : (g + 1) * TOK, :]
         fill_ref[:, g * HEAD : (g + 1) * HEAD] = (a[:, :HEAD] / a[:, HEAD:]).astype(jnp.bfloat16)
@@ -333,10 +365,17 @@
     send_dq.wait_send()
     send_dkv.wait_send()
     for piece in (0, 1):
-        for dx, dz in near[1:] + far:
+        for dx, dz in direct:
             chip_copy(piece, dx, dz).wait_send()
+        for dx, dz in passed:
+            onward_copy(piece, dx, dz).wait_send()
         for dx, dz in near + far:
             core_copy(piece, dx, dz).wait_send()
+
+
+def store(*refs):
+    for source, target in zip(refs[:3], refs[3:]):
+        target[...] = source[...]
 
 
 def on_device(*args):
@@ -349,13 +388,14 @@
     vmem = pl.BlockSpec(memory_space=pltpu.VMEM)
     bf16 = jnp.bfloat16
     dma = pltpu.SemaphoreType.DMA
-    return pl.pallas_call(
+    shapes = (
+        jax.ShapeDtypeStruct((TOK, GROUP * HEAD), bf16),
+        jax.ShapeDtypeStruct((2, PAGE, 4 * HEAD), bf16),
+        jax.ShapeDtypeStruct((ROWS, STEPS, 2 * GROUP * HEAD), bf16),
+    )
+    results = pl.pallas_call(
         kernel,
-        out_shape=(
-            jax.ShapeDtypeStruct((TOK, GROUP * HEAD), bf16),
-            jax.ShapeDtypeStruct((2, PAGE, 4 * HEAD), bf16),
-            jax.ShapeDtypeStruct((ROWS, STEPS, 2 * GROUP * HEAD), bf16),
-        ),
+        out_shape=shapes,
         in_specs=[any_spec, any_spec, any_spec, smem, smem, any_spec, any_spec, any_spec, smem]
         + [vmem] * 3,
         out_specs=(vmem,) * 3,
@@ -368,7 +408,7 @@
             pltpu.VMEM((GROUP * TOK, 2 * HEAD), jnp.float32),
             pltpu.VMEM((GROUP * TOK, 1), jnp.float32),
             pltpu.VMEM((8, CHIP), jnp.float32),
-            pltpu.VMEM((BLOCK, CHIP), jnp.float32),
+            pltpu.VMEM((2 * BLOCK, CHIP), jnp.float32),
             pltpu.VMEM((2, ROWS, STEPS, GROUP * HEAD), bf16),
             pltpu.VMEM((2, ROWS, STEPS, 2 * HEAD), bf16),
             pltpu.VMEM((ROWS, SLOTS, 4 * HEAD), bf16),
@@ -402,6 +442,12 @@
         jnp.asarray(np.sin(angles).astype(np.float32)),
         jnp.asarray(np.tile(freq[None, :], (8, 1))),
     )
+    return pl.pallas_call(
+        store,
+        out_shape=shapes,
+        in_specs=[vmem] * 3,
+        out_specs=(vmem,) * 3,
+    )(*results)
 
 
 def solution(mesh):

time: 62.7 us -> 56.8 us (0.906)
  local copies, waits for them, and re-layouts: 5.04 us -> 0 us
  Pallas kernels: 56.1 us -> 55.3 us
    unnamed x3 -> x0, local copies, waits for them, and re-layouts: 5.04 us -> none
    pallas_call x1 -> x2, Pallas kernels: 56.1 us -> 55.3 us  [the longest x1 53.3 us: on_device(): pl.pallas_call(kernel, out_shape=shapes, in_specs=[any_spec, any_spec, an...]
where the time goes in v2:
time: 56.8 us; the launch traced here: 56.6 us
  Pallas kernels  55.3 us (97%)
  between operations  1.29 us (2%)
    pallas_call x1, Pallas kernels, on_device(): pl.pallas_call(kernel, out_shape=shapes, in_specs=[any_spec, any_spec, an...  53.3 us
    pallas_call x1, Pallas kernels, on_device(): pl.pallas_call(store, out_shape=shapes, in_specs=[vmem] * 3, out_specs=(v...  2.01 us

profile of v2, /device:TPU:1, one launch (start us, length us, event | category | flops | bytes accessed | tf_op | source)
XLA Modules:
  0.0 56.6 jit_solution(13184211848767079208)
XLA Ops:
  1.3 53.3 %shard_map.139 = (bf16[256,1024]{1,0:T(8,128)(2,1)}, bf16[2,64,512]{2,1,0:T(8,128)(2,1)}, bf16[8,4,2048]{2,1,0:T(4,128)(2,1)}) custom-call(bf16[256,1024]{1,0:T(8,128)(2,1)} %sq_hbm.1, bf16[256,256]{1,0:T(8,128)(2,1)} %skv_hbm.1, bf16[256,256]{1,0:T(8,128)(2,1)} %ekv_hbm.1, s32[1]{0:T(128)S(6)} %copy.15.start_ref, s32[64]{0:T(128)} %page_ref.1, ...), custom_call_target="tpu_custom_call" | custom-call | flops 10737418240 | bytes 10485760 | tf_op jit(solution)/shard_map/pallas_call | solution.py:396
  54.6 2.0 %shard_map.140 = (bf16[256,1024]{1,0:T(8,128)(2,1)}, bf16[2,64,512]{2,1,0:T(8,128)(2,1)}, bf16[8,4,2048]{2,1,0:T(4,128)(2,1)}) custom-call(bf16[256,1024]{1,0:T(8,128)(2,1)} %get-tuple-element.6.refs_0_, bf16[2,64,512]{2,1,0:T(8,128)(2,1)} %get-tuple-element.7.refs_1_, bf16[8,4,2048]{2,1,0:T(4,128)(2,1)} %get-tuple-element.8.refs_2_), custom_call_target="tpu_custom_call" | custom-call | tf_op jit(solution)/shard_map/pallas_call | solution.py:445

commit v3 on v2

--- a/solution.py
+++ b/solution.py
@@ -135,6 +135,19 @@
     for row in range(ROWS):
         cache_copy(row).start()
 
+    def send(piece):
+        for dx, dz in near[1:]:
+            chip_copy(piece, dx, dz).start()
+        core_copy(piece, 0, 0).start()
+
+    send_dq = remote(dq_hbm.at[other], dq.at[sec], d_send.at[0], d_recv.at[0], partner)
+    send_dkv = remote(dkv_hbm.at[other], dkv.at[sec], d_send.at[1], d_recv.at[1], partner)
+    load_e.wait()
+    pl.semaphore_wait(barrier, 6)
+    send_dkv.start()
+    send_dq.start()
+    send(0)
+
     lane = lax.broadcasted_iota(jnp.int32, (1, HEAD), 1)
     sign = jnp.where(lane < HEAD // 2, -1.0, 1.0)
     freq = freq_ref[0:1, :]
@@ -150,16 +163,7 @@
     near_keys[fresh_rows, :HEAD] = turned
     near_keys[fresh_rows, HEAD:] = skv[:, HEAD:]
 
-    load_e.wait()
-    pl.semaphore_wait(barrier, 6)
-    send_dq = remote(dq_hbm.at[other], dq.at[sec], d_send.at[0], d_recv.at[0], partner)
-    send_dkv = remote(dkv_hbm.at[other], dkv.at[sec], d_send.at[1], d_recv.at[1], partner)
-    send_dkv.start()
-    send_dq.start()
-    for piece in (0, 1):
-        for dx, dz in near[1:]:
-            chip_copy(piece, dx, dz).start()
-        core_copy(piece, 0, 0).start()
+    send(1)
     for piece in (0, 1):
         chip_copy(piece, 0, 2).start()
 

time: 56.8 us -> 56.8 us (level)
  no operation moved by 1% of the time
where the time goes in v3:
time: 56.8 us; the launch traced here: 56.6 us
  Pallas kernels  55.3 us (97%)
  between operations  1.29 us (2%)
    pallas_call x1, Pallas kernels, on_device(): pl.pallas_call(kernel, out_shape=shapes, in_specs=[any_spec, any_spec, an...  53.3 us
    pallas_call x1, Pallas kernels, on_device(): pl.pallas_call(store, out_shape=shapes, in_specs=[vmem] * 3, out_specs=(v...  2.01 us

profile of v3, /device:TPU:1, one launch (start us, length us, event | category | flops | bytes accessed | tf_op | source)
XLA Modules:
  0.0 56.6 jit_solution(7278440729279321509)
XLA Ops:
  1.3 53.3 %shard_map.139 = (bf16[256,1024]{1,0:T(8,128)(2,1)}, bf16[2,64,512]{2,1,0:T(8,128)(2,1)}, bf16[8,4,2048]{2,1,0:T(4,128)(2,1)}) custom-call(bf16[256,1024]{1,0:T(8,128)(2,1)} %sq_hbm.1, bf16[256,256]{1,0:T(8,128)(2,1)} %skv_hbm.1, bf16[256,256]{1,0:T(8,128)(2,1)} %ekv_hbm.1, s32[1]{0:T(128)S(6)} %copy.15.start_ref, s32[64]{0:T(128)} %page_ref.1, ...), custom_call_target="tpu_custom_call" | custom-call | flops 10737418240 | bytes 10485760 | tf_op jit(solution)/shard_map/pallas_call | solution.py:400
  54.6 2.0 %shard_map.140 = (bf16[256,1024]{1,0:T(8,128)(2,1)}, bf16[2,64,512]{2,1,0:T(8,128)(2,1)}, bf16[8,4,2048]{2,1,0:T(4,128)(2,1)}) custom-call(bf16[256,1024]{1,0:T(8,128)(2,1)} %get-tuple-element.6.refs_0_, bf16[2,64,512]{2,1,0:T(8,128)(2,1)} %get-tuple-element.7.refs_1_, bf16[8,4,2048]{2,1,0:T(4,128)(2,1)} %get-tuple-element.8.refs_2_), custom_call_target="tpu_custom_call" | custom-call | tf_op jit(solution)/shard_map/pallas_call | solution.py:449

commit v4 on v2

--- a/solution.py
+++ b/solution.py
@@ -268,7 +268,7 @@
     def rows_of(i):
         return (near_keys, far_keys)[i // 4], slice(i % 4 * CHIP, (i % 4 + 1) * CHIP)
 
-    def attend(chips, size, event=None):
+    def attend(chips, size, event=None, when=2):
         blocks = GROUP * TOK // size
 
         def lines_of(block):
@@ -282,7 +282,7 @@
 
         def step(block, carry):
             if event is not None:
-                pl.when(block == 2)(event)
+                pl.when(block == when)(event)
             lines = lines_of(block)
             m, a = top[lines, :], acc[lines, :]
             s = scores[:size, :]
@@ -308,8 +308,7 @@
     acc[...] = jnp.zeros_like(acc)
     top[...] = jnp.full_like(top, NEG)
     from_sibling(near[:1])
-    attend((0,), 2 * BLOCK)
-    pass_on(near[2:])
+    attend((0,), 2 * BLOCK, lambda: pass_on(near[2:]), 1)
     from_sibling(near[1:])
 
     def send_across():
@@ -320,8 +319,7 @@
     attend((1, 2, 3), BLOCK, send_across)
     pass_on(far[1:3])
     from_sibling(far[:3])
-    attend((4, 5, 6), BLOCK)
-    pass_on(far[3:])
+    attend((4, 5, 6), BLOCK, lambda: pass_on(far[3:]))
     from_sibling(far[3:])
 
     own_page = (ctx * 2 + sec) * 2

time: 56.8 us -> 54.8 us (0.965)
  Pallas kernels: 55.3 us -> 53.3 us
    pallas_call x1, Pallas kernels: 53.3 us -> 51.3 us  [on_device(): pl.pallas_call(kernel, out_shape=shapes, in_specs=[any_spec, any_spec, an...]
where the time goes in v4:
time: 54.8 us; the launch traced here: 54.6 us
  Pallas kernels  53.3 us (97%)
  between operations  1.29 us (2%)
    pallas_call x1, Pallas kernels, on_device(): pl.pallas_call(kernel, out_shape=shapes, in_specs=[any_spec, any_spec, an...  51.3 us
    pallas_call x1, Pallas kernels, on_device(): pl.pallas_call(store, out_shape=shapes, in_specs=[vmem] * 3, out_specs=(v...  2.01 us

profile of v4, /device:TPU:1, one launch (start us, length us, event | category | flops | bytes accessed | tf_op | source)
XLA Modules:
  0.0 54.6 jit_solution(10716316840676474071)
XLA Ops:
  1.3 51.3 %shard_map.139 = (bf16[256,1024]{1,0:T(8,128)(2,1)}, bf16[2,64,512]{2,1,0:T(8,128)(2,1)}, bf16[8,4,2048]{2,1,0:T(4,128)(2,1)}) custom-call(bf16[256,1024]{1,0:T(8,128)(2,1)} %sq_hbm.1, bf16[256,256]{1,0:T(8,128)(2,1)} %skv_hbm.1, bf16[256,256]{1,0:T(8,128)(2,1)} %ekv_hbm.1, s32[1]{0:T(128)S(6)} %copy.15.start_ref, s32[64]{0:T(128)} %page_ref.1, ...), custom_call_target="tpu_custom_call" | custom-call | flops 10737418240 | bytes 10485760 | tf_op jit(solution)/shard_map/pallas_call | solution.py:394
  52.6 2.0 %shard_map.140 = (bf16[256,1024]{1,0:T(8,128)(2,1)}, bf16[2,64,512]{2,1,0:T(8,128)(2,1)}, bf16[8,4,2048]{2,1,0:T(4,128)(2,1)}) custom-call(bf16[256,1024]{1,0:T(8,128)(2,1)} %get-tuple-element.6.refs_0_, bf16[2,64,512]{2,1,0:T(8,128)(2,1)} %get-tuple-element.7.refs_1_, bf16[8,4,2048]{2,1,0:T(4,128)(2,1)} %get-tuple-element.8.refs_2_), custom_call_target="tpu_custom_call" | custom-call | tf_op jit(solution)/shard_map/pallas_call | solution.py:443
